TPU v7x, 512 devices: a whole 4x4x16 slice. The times are simulated.
512 devices in a mesh: grp: 16 (over y, x), node: 32 (over z, core).
Axes of the slice: x: 4, y: 4, z: 16, core: 2. Of those that a mesh axis runs over, the one named last changes fastest.
Arguments:
- damage: bfloat16 [4096, 65536], P('grp', 'node'), may hold values from -6 to 6
- basis_table: bfloat16 [4096, 512], P('grp'), may hold values from -6 to 6
- train_ids: int32 [4096], P('grp'), may hold values from 0 to 4095, each once
- counts: int32 [16], replicated, may hold values from 64 to 256
- new_table: bfloat16 [2048, 512], replicated, may hold values from -6 to 6
- new_ids: int32 [1024], replicated, may hold values from 0 to 2047
Outputs:
- surrogate: bfloat16 [1024, 65536], P('grp', 'node')
- peak: float32 [1024], P('grp')
- spread: float32 [1024], P('grp')
Inputs may be any that keep to these rules, and one draw needn't show every extreme that they name: `train_ids`: each row of basis_table is named by exactly one slot.
All inputs are finite; a program needn't handle non-finite values.
Results may differ from a plain program's by a relative error of at most 0.0085.
Values may be sent and summed in bfloat16 or wider, within the bound.
A program may use at most 64 MiB of HBM per device.

v0:
```python
import jax
import jax.numpy as jnp
from jax import lax
from jax.sharding import PartitionSpec as P


def cut_along(value, dim, size):
    before, after = (value.shape[:dim], value.shape[dim + 1 :])
    return jnp.moveaxis(value.reshape(*before, size, -1, *after), dim, 0)


def sent_and_summed(value, axis, dim):
    blocks = cut_along(value, dim, lax.axis_size(axis))
    arrived = lax.all_to_all(blocks, axis, split_axis=0, concat_axis=0, tiled=True)
    return arrived.astype(jnp.float32).sum(axis=0)


def from_everyone(value, axis):
    size = lax.axis_size(axis)
    return lax.all_to_all(
        jnp.broadcast_to(value[None], (size, *value.shape)), axis, 0, 0, tiled=True
    )


def in_order(blocks, dim):
    dims = list(blocks.shape[1:])
    dims[dim] *= blocks.shape[0]
    return jnp.moveaxis(blocks, 0, dim).reshape(dims)


def gather_directly(value, axis, dim):
    blocks = from_everyone(value, axis)
    return in_order(blocks, dim)


def collected_together(value, axis):
    leaves = jax.tree.leaves(value)
    sequence = sorted(range(len(leaves)), key=lambda k: -leaves[k].size)
    width = (1, *leaves[sequence[0]].shape)[-1]
    lines = [
        jnp.pad(leaves[k].reshape(-1), (0, -leaves[k].size % width)).reshape(-1, width)
        for k in sequence
    ]
    both, at, found = (from_everyone(jnp.concatenate(lines), axis), 0, {})
    for k, line in zip(sequence, lines):
        section = both[:, at : at + len(line)].reshape(len(both), -1)
        found[k] = section[:, : leaves[k].size].reshape(-1, *leaves[k].shape)
        at += len(line)
    numbers = iter(range(len(leaves)))
    return jax.tree.map(lambda _: found[next(numbers)], value)


def folded_in_pairs(pieces, combine):
    while len(jax.tree.leaves(pieces)[0]) > 1:
        pieces = jax.vmap(combine)(
            *(jax.tree.map(lambda part: part[side::2], pieces) for side in (0, 1))
        )
    return jax.tree.map(lambda part: part[0], pieces)


def joined_all(value, axis, combine):
    pieces = collected_together(value, axis)
    return folded_in_pairs(pieces, combine)


def combine_stats(first, second):
    return (first[0] + second[0], jnp.maximum(first[1], second[1]))


def local(damage, basis_table, train_ids, counts, new_table, new_ids):
    slot_count = damage.shape[0]
    node_cells = damage.shape[1]
    group_index = lax.axis_index("grp")
    group_total = lax.axis_size("grp")
    total_nodes = node_cells * lax.axis_size("node")
    per_group = new_ids.shape[0] // group_total
    sample_total = jnp.sum(counts).astype(jnp.float32)
    basis_whole, ids_whole = (
        lax.all_gather(basis_table, "grp", axis=0, tiled=True),
        lax.all_gather(train_ids, "grp", axis=0, tiled=True),
    )
    my_slot_ids = lax.dynamic_slice_in_dim(ids_whole, group_index * slot_count, slot_count, 0)
    live_slot = jnp.arange(slot_count, dtype=jnp.int32) < counts[group_index]
    chosen = jnp.take(basis_whole, my_slot_ids, axis=0)
    weighted = jnp.where(live_slot[:, None], chosen, jnp.zeros_like(chosen))
    my_ids = lax.dynamic_slice_in_dim(new_ids, group_index * per_group, per_group, 0)
    new_rows = jnp.take(new_table, my_ids, axis=0)
    term_cols = weighted
    product = lax.dot_general(
        term_cols, damage, (((0,), (0,)), ((), ())), preferred_element_type=jnp.float32
    )
    coef_share = sent_and_summed((product / sample_total).astype(jnp.bfloat16), "grp", 0)
    term_cols = new_rows
    values = jnp.dot(
        term_cols,
        gather_directly(coef_share.astype(jnp.bfloat16), "grp", 0),
        preferred_element_type=jnp.float32,
    )
    local_square = jnp.sum(values * values, axis=1)
    local_peak = jnp.max(values, axis=1)
    squares, peak_value = joined_all((local_square, local_peak), "node", combine_stats)
    surrogate = values.astype(jnp.bfloat16)
    spread = jnp.sqrt(squares / total_nodes + 1e-06)
    return (surrogate, peak_value, spread)


def solution(mesh):
    placed = (P("grp", "node"), P("grp", None), P("grp"), P(), P(), P())
    return jax.shard_map(
        local,
        mesh=mesh,
        in_specs=placed,
        out_specs=(P("grp", "node"), P("grp"), P("grp")),
        check_vma=False,
    )
```

profile of v0, /device:TPU:1, one launch (start us, length us, event | category | flops | bytes accessed | tf_op | source)
XLA Modules:
  0.0 196.4 jit_solution(9732886169708049763)
XLA Ops:
  7.2 0.0 copy-start
  7.2 0.0 copy-start.1
  7.2 0.0 all-gather.3.cloned.1.call-start
  7.2 0.7 all-gather.3.cloned.1.call-update
  7.9 1.3 reduce_sum.30
  9.2 1.2 dynamic_slice.10
  11.1 19.1 %all-gather = s32[16,1,256]{2,1,0:T(1,128)S(1)} all-gather(s32[1,1,256]{2,1,0:T(1,128)} %bitcast.23), channel_id=1, replica_groups=mesh['grp'=16,'node'=32] {'grp'}, dimensions={0}, use_global_device_ids=true | all-gather | bytes 17408 | tf_op jit(solution)/shard_map/all_gather | solution.py:80
  30.2 0.7 compare_and_fusion
  30.9 52.3 %all-gather.3.cloned.1.call-done = bf16[4096,512]{1,0:T(8,128)(2,1)} async-done(((bf16[256,512]{1,0:T(8,128)(2,1)}), bf16[4096,512]{1,0:T(8,128)(2,1)}) %all-gather.3.cloned.1.call-update) | async-done | bytes 4194320 | tf_op jit(solution)/shard_map/all_gather | solution.py:79
  83.2 3.9 %gather_fusion.1 = bf16[256,512]{1,0:T(8,128)(2,1)S(1)} fusion(bf16[4096,512]{1,0:T(8,128)(2,1)} %all-gather.3.cloned.1.call-done, s32[1024]{0:T(1024)S(1)} %pad_clamp_fusion), kind=kCustom, calls=%fused_computation.1 | custom fusion | bytes 525312 | tf_op jit(solution)/shard_map/jit(_take)/gather | solution.py:84
  87.2 0.0 copy-done.1
  87.2 0.9 divide_convert_fusion
  88.0 32.2 %all_to_all.15 = bf16[16,32,2048]{2,1,0:T(8,128)(2,1)} all-to-all(bf16[16,32,2048]{2,1,0:T(8,128)(2,1)S(1)} %bitcast.15), channel_id=1, replica_groups=mesh['grp'=16,'node'=32] {'grp'}, dimensions={0} | all-to-all | bytes 4194304 | tf_op jit(solution)/shard_map/all_to_all | solution.py:14
  120.3 2.0 %reduce_sum.31 = bf16[32,2048]{1,0:T(8,128)(2,1)S(1)} reduce(bf16[16,32,2048]{2,1,0:T(8,128)(2,1)} %all_to_all.15, bf16[]{:T(256)} %constant.53.clone.1), dimensions={0}, to_apply=%region_1.2 | reduce | flops 983040 | bytes 2228226 | tf_op jit(solution)/shard_map/reduce_sum | solution.py:15
  122.3 1.6 broadcast_in_dim.56
  123.8 4.4 %all-to-all-start.1 = ((bf16[16,32,2048]{2,1,0:T(8,128)(2,1)}), bf16[16,32,2048]{2,1,0:T(8,128)(2,1)}, u32[]{:S(2)}, u32[]{:S(2)}) async-start(bf16[16,32,2048]{2,1,0:T(8,128)(2,1)} %broadcast_in_dim.56), calls=%async_computation.1 | async-start | bytes 4194304 | tf_op jit(solution)/shard_map/all_to_all | solution.py:20
  128.2 0.8 compare_and_fusion.1
  129.0 0.0 copy-done
  129.0 0.7 gather_fusion
  129.7 25.8 %all-to-all-done.1 = bf16[16,32,2048]{2,1,0:T(8,128)(2,1)} async-done(((bf16[16,32,2048]{2,1,0:T(8,128)(2,1)}), bf16[16,32,2048]{2,1,0:T(8,128)(2,1)}, u32[]{:S(2)}, u32[]{:S(2)}) %all-to-all-start.1) | async-done | bytes 2097184 | tf_op jit(solution)/shard_map/all_to_all | solution.py:20
  155.5 2.9 %multiply_reduce_fusion = (f32[64]{0:T(128)S(1)}, f32[64]{0:T(128)S(1)}, bf16[64,2048]{1,0:T(8,128)(2,1)}) fusion(bf16[512,2048]{1,0:T(8,128)(2,1)} %bitcast.4, bf16[64,512]{1,0:T(8,128)(2,1)S(1)} %gather_fusion, pred[64]{0:T(512)(128)(4,1)S(1)} %get-tuple-element.5), kind=kOutput, calls=%fused_computation.3 | convolution fusion | flops 134774656 | bytes 2425408 | tf_op jit(solution)/shard_map/dot_general | solution.py:94
  158.5 0.1 reshape.71
  158.6 28.3 %all_to_all.16 = f32[32,1,128]{2,1,0:T(1,128)S(1)} all-to-all(f32[32,1,128]{2,1,0:T(1,128)S(1)} %reshape.71), channel_id=1, replica_groups=mesh['grp'=16,'node'=32] {'node'}, dimensions={0} | all-to-all | bytes 32768 | tf_op jit(solution)/shard_map/all_to_all | solution.py:20
  186.8 0.5 broadcast.26
  187.3 0.7 reduce.1
  188.0 0.1 reshape.72
  188.5 0.5 sqrt_bitcast_fusion
  189.0 0.5 maximum_bitcast_fusion
  (29 shorter events, 0.4 us)
Async XLA Ops:
  7.2 121.9 %copy-start = (bf16[2048,512]{1,0:T(8,128)(2,1)S(1)}, bf16[2048,512]{1,0:T(8,128)(2,1)}, u32[]{:S(2)}) copy-start(bf16[2048,512]{1,0:T(8,128)(2,1)} %param.10) | copy-start | bytes 6291460
  7.2 80.0 %copy-start.1 = (bf16[256,2048]{1,0:T(8,128)(2,1)S(1)}, bf16[256,2048]{1,0:T(8,128)(2,1)}, u32[]{:S(2)}) copy-start(bf16[256,2048]{1,0:T(8,128)(2,1)} %param.6) | copy-start | bytes 3145732
  7.2 76.0 %all-gather.3.cloned.1.call-start = ((), (), s32[]{:S(2)}) async-start(), calls=%async_computation.3 | async-start | bytes 4456448 | tf_op jit(solution)/shard_map/all_gather | solution.py:79
  123.8 31.7 %all-to-all-start.1 = ((bf16[16,32,2048]{2,1,0:T(8,128)(2,1)}), bf16[16,32,2048]{2,1,0:T(8,128)(2,1)}, u32[]{:S(2)}, u32[]{:S(2)}) async-start(bf16[16,32,2048]{2,1,0:T(8,128)(2,1)} %broadcast_in_dim.56), calls=%async_computation.1 | async-start | bytes 4194304 | tf_op jit(solution)/shard_map/all_to_all | solution.py:20
Sparse Core Ops, SparseCore 0:
  11.0 72.1 all-gather.2
where the time goes:
time: 197 us; the launch traced here: 196 us
  blocking collectives  79.6 us (40%)
  waiting for transfers between devices  78.7 us (40%)
  between operations  14.8 us (8%)
  local copies, waits for them, and re-layouts  8.48 us (4%)
  other arithmetic  6.56 us (3%)
  starting transfers between devices  4.46 us (2%)
  matrix products  3.8 us (2%)
    all_gather x1, waiting for transfers between devices, local(): lax.all_gather(basis_table, 'grp', axis=0, tiled=True)  52.3 us
    all_to_all x1, blocking collectives, sent_and_summed(): lax.all_to_all(blocks, axis, split_axis=0, concat_axis=0, tiled=True)  32.2 us
    all_to_all x1, blocking collectives, from_everyone(): lax.all_to_all(jnp.broadcast_to(value[None], (size, *value.shape)), axis,...  28.3 us
    all_to_all x1, waiting for transfers between devices, from_everyone(): lax.all_to_all(jnp.broadcast_to(value[None], (size, *value.shape)), axis,...  25.8 us
    all_gather x1, blocking collectives, local(): lax.all_gather(train_ids, 'grp', axis=0, tiled=True)  19.1 us
    all_to_all x1, starting transfers between devices, from_everyone(): lax.all_to_all(jnp.broadcast_to(value[None], (size, *value.shape)), axis,...  4.42 us
  transfers between devices with their start and end apart: 2, of which 2 were waited for; matrix products, arithmetic and copies ran while one was open for 2% of the time, Pallas kernels for 0%

commit v1 on v0

v1 whole, which is shorter than its diff:
```python
import functools

import jax
import jax.numpy as jnp
from jax import lax
from jax.experimental import pallas as pl
from jax.experimental.pallas import tpu as pltpu
from jax.sharding import PartitionSpec as P

MESH = pl.DeviceIdType.MESH
F32 = jnp.float32
BF16 = jnp.bfloat16


def side_of(count):
    side = 1
    while side * side < count:
        side *= 2
    return side


def near_first(count):
    order = [0]
    for step in range(1, count // 2 + 1):
        order += [step, -step]
    return order[:count]


def kernel(
    sizes,
    damage_hbm, basis_hbm, ids_ref, counts_ref, table_hbm, new_ids_ref,
    out_ref, peak_ref, spread_ref,
    damage, basis, table, onehot, parts, weights, partial, first_in, half, second_in,
    coef, pick, chosen, sending, field, stat_own, stat_pair, stat_all,
    local_sem, part_send, part_recv, weight_send, weight_recv, twin_send, twin_recv,
    first_send, first_recv, second_send, second_recv, field_send, field_recv,
    stat_send, stat_recv,
):
    groups, nodes, slots, terms, cells, samples, rows = sizes
    edge = side_of(groups)
    depth = nodes // 2
    chunk = terms // nodes
    block = cells // groups
    share = samples // groups
    stages = partial.shape[0]
    per_stage = depth // stages
    lines = per_stage * chunk
    offsets = near_first(depth)

    grp = lax.axis_index("grp")
    node = lax.axis_index("node")
    col, row = lax.rem(grp, edge), lax.div(grp, edge)
    level, core = lax.div(node, 2), lax.rem(node, 2)
    twin = level * 2 + (1 - core)

    def grp_peer(step):
        return lax.rem(grp + step + groups, groups)

    def level_peer(step):
        return lax.rem(level + step + depth, depth) * 2 + core

    def in_row(step):
        return lax.rem(col + step, edge)

    def in_col(step):
        return lax.rem(row + step, edge)

    sent = []

    def send(src, dst, send_sem, recv_sem, to):
        copy = pltpu.make_async_remote_copy(
            src_ref=src, dst_ref=dst, send_sem=send_sem, recv_sem=recv_sem,
            device_id=to, device_id_type=MESH,
        )
        copy.start()
        sent.append(copy)

    def arrived(dst, send_sem, recv_sem):
        pltpu.make_async_remote_copy(
            src_ref=dst, dst_ref=dst, send_sem=send_sem, recv_sem=recv_sem,
            device_id=(grp, twin), device_id_type=MESH,
        ).wait_recv()

    load_basis = pltpu.make_async_copy(basis_hbm, basis, local_sem.at[0])
    load_damage = pltpu.make_async_copy(damage_hbm, damage, local_sem.at[1])
    load_table = pltpu.make_async_copy(table_hbm, table, local_sem.at[2])
    load_basis.start()
    load_damage.start()
    load_table.start()

    barrier = pltpu.get_barrier_semaphore()
    for step in range(1, groups):
        pl.semaphore_signal(barrier, inc=1, device_id=(grp_peer(step), node), device_id_type=MESH)
    for step in range(1, depth):
        pl.semaphore_signal(barrier, inc=1, device_id=(grp, level_peer(step)), device_id_type=MESH)
    pl.semaphore_signal(barrier, inc=1, device_id=(grp, twin), device_id_type=MESH)

    ids = ids_ref[...]
    line = lax.broadcasted_iota(jnp.int32, (slots, slots), 0)
    wanted = jnp.broadcast_to(ids, (slots, slots)) - line

    @pl.loop(0, groups)
    def _(g):
        onehot[g] = jnp.where(wanted == g * slots, 1.0, 0.0).astype(BF16)

    total = jnp.int32(0)
    for g in range(groups):
        total = total + counts_ref[g]
    live = counts_ref[grp]
    total = total.astype(F32)

    load_basis.wait()
    pick_terms = lax.broadcasted_iota(jnp.int32, (chunk, terms), 1) - node * chunk
    pick_terms = pick_terms == lax.broadcasted_iota(jnp.int32, (chunk, terms), 0)
    parts[grp] = lax.dot_general(
        jnp.where(pick_terms, 1.0, 0.0).astype(BF16), basis[...],
        (((1,), (1,)), ((), ())), preferred_element_type=F32,
    ).astype(BF16)

    pl.semaphore_wait(barrier, groups - 1 + depth)

    for step in range(1, groups):
        send(parts.at[grp], parts.at[grp], part_send.at[step], part_recv.at[step], (grp_peer(step), node))

    mine = jnp.dot(parts[grp], onehot[grp], preferred_element_type=F32)
    for step in range(1, groups):
        source = grp_peer(-step)
        arrived(parts.at[source], part_send.at[step], part_recv.at[step])
        mine = mine + jnp.dot(parts[source], onehot[source], preferred_element_type=F32)
    slot = lax.broadcasted_iota(jnp.int32, (chunk, slots), 1)
    weights[0, 0] = jnp.where(slot < live, mine, 0.0).astype(BF16)

    send(weights.at[0, 0], weights.at[0, 1], twin_send.at[0], twin_recv.at[0], (grp, twin))
    for k in range(1, depth):
        send(weights.at[0, 0], weights.at[k, 0], weight_send.at[k], weight_recv.at[k], (grp, level_peer(-offsets[k])))

    def pass_on(stage):
        for k in range(stage * per_stage, (stage + 1) * per_stage):
            if k:
                arrived(weights.at[k, 0], weight_send.at[k], weight_recv.at[k])
                send(weights.at[k, 0], weights.at[k, 1], twin_send.at[k], twin_recv.at[k], (grp, twin))

    def project(stage):
        for k in range(stage * per_stage, (stage + 1) * per_stage):
            arrived(weights.at[k, 1], twin_send.at[k], twin_recv.at[k])
        left = weights[stage * per_stage : (stage + 1) * per_stage].reshape(2 * lines, slots)
        for r in range(edge):
            wide = edge * block
            product = jnp.dot(left, damage[:, r * wide : (r + 1) * wide], preferred_element_type=F32).astype(BF16)
            for c in range(edge):
                piece = product[:, c * block : (c + 1) * block]
                partial[stage, 0, c, r] = piece[:lines]
                partial[stage, 1, r, c] = piece[lines:]
        for step in range(1, edge):
            send(
                partial.at[stage, 0, in_row(step)], first_in.at[stage, 0, step - 1],
                first_send.at[stage, 0, step], first_recv.at[stage, 0, step], (row * edge + in_row(step), node),
            )
            send(
                partial.at[stage, 1, in_col(step)], first_in.at[stage, 1, step - 1],
                first_send.at[stage, 1, step], first_recv.at[stage, 1, step], (in_col(step) * edge + col, node),
            )

    def middle(stage):
        for side, own in ((0, col), (1, row)):
            for step in range(1, edge):
                arrived(first_in.at[stage, side, step - 1], first_send.at[stage, side, step], first_recv.at[stage, side, step])
            for q in range(edge):
                amount = partial[stage, side, own, q].astype(F32)
                for step in range(1, edge):
                    amount = amount + first_in[stage, side, step - 1, q].astype(F32)
                half[stage, side, q] = amount.astype(BF16)
        for step in range(1, edge):
            send(
                half.at[stage, 0, in_col(step)], second_in.at[stage, 0, step - 1],
                second_send.at[stage, 0, step], second_recv.at[stage, 0, step], (in_col(step) * edge + col, node),
            )
            send(
                half.at[stage, 1, in_row(step)], second_in.at[stage, 1, step - 1],
                second_send.at[stage, 1, step], second_recv.at[stage, 1, step], (row * edge + in_row(step), node),
            )

    def finish(stage):
        for side, own in ((0, row), (1, col)):
            for step in range(1, edge):
                arrived(second_in.at[stage, side, step - 1], second_send.at[stage, side, step], second_recv.at[stage, side, step])
            amount = half[stage, side, own].astype(F32)
            for step in range(1, edge):
                amount = amount + second_in[stage, side, step - 1].astype(F32)
            amount = (amount / total).astype(BF16)
            for i in range(per_stage):
                at = side * per_stage + i
                k, other = stage * per_stage + at // 2, at % 2
                owner = lax.rem(level + offsets[k] + depth, depth) * 2 + (1 - core if other else core)
                coef[pl.ds(pl.multiple_of(owner * chunk, chunk), chunk), :] = amount[i * chunk : (i + 1) * chunk]

    def choose(part):
        width = samples // edge
        wanted_row = new_ids_ref[:, part * width : (part + 1) * width].astype(F32)
        wanted_row = jnp.broadcast_to(wanted_row, (128, width)).T
        lane = lax.broadcasted_iota(jnp.int32, (width, 128), 1).astype(F32)
        wanted_row = wanted_row - lane
        for q in range(rows // 128):
            pick[:, q * 128 : (q + 1) * 128] = jnp.where(wanted_row == q * 128.0, 1.0, 0.0).astype(BF16)
        chosen[part * width : (part + 1) * width, :] = jnp.dot(
            pick[...], table[...], preferred_element_type=F32
        ).astype(BF16)

    load_damage.wait()
    pass_on(0)
    project(0)
    load_table.wait()
    parts_done = 0
    for stage in range(stages):
        if stage + 1 < stages:
            pass_on(stage + 1)
            project(stage + 1)
        while parts_done < edge * (stage + 1) // stages:
            choose(parts_done)
            parts_done += 1
        middle(stage)
        if stage:
            finish(stage - 1)
    finish(stages - 1)

    for r in range(edge):
        to_row = in_col(r)
        wide = edge * share
        values = jnp.dot(
            chosen[pl.ds(pl.multiple_of(to_row * wide, wide), wide), :], coef[...], preferred_element_type=F32
        ).astype(BF16)
        sending[r] = values.reshape(edge, share, block)
        for c in range(edge):
            to_col = in_row(c)
            here = pl.ds(pl.multiple_of(grp * block, block), block)
            if r == 0 and c == 0:
                field[:, here] = sending[r, to_col]
            else:
                at = r * edge + c
                send(
                    sending.at[r, to_col], field.at[:, here], field_send.at[at], field_recv.at[at],
                    (to_row * edge + to_col, node),
                )

    squares = jnp.zeros((share, block), F32)
    peak = jnp.full((share, block), -jnp.inf, F32)
    for r in range(edge):
        for c in range(edge):
            source = lax.rem(row + edge - r, edge) * edge + lax.rem(col + edge - c, edge)
            here = pl.ds(pl.multiple_of(source * block, block), block)
            if r or c:
                arrived(field.at[:, here], field_send.at[r * edge + c], field_recv.at[r * edge + c])
            piece = field[:, here].astype(F32)
            squares = squares + piece * piece
            peak = jnp.maximum(peak, piece)
    write = pltpu.make_async_copy(field, out_ref, local_sem.at[3])
    write.start()

    stat_own[0:1, :share] = jnp.sum(squares.T, axis=0, keepdims=True)
    stat_own[1:2, :share] = jnp.max(peak.T, axis=0, keepdims=True)
    send(stat_own, stat_pair, stat_send.at[0], stat_recv.at[0], (grp, twin))
    arrived(stat_pair, stat_send.at[0], stat_recv.at[0])
    stat_all[level, 0:1, :] = stat_own[0:1, :] + stat_pair[0:1, :]
    stat_all[level, 1:2, :] = jnp.maximum(stat_own[1:2, :], stat_pair[1:2, :])
    for step in range(1, depth):
        send(stat_all.at[level], stat_all.at[level], stat_send.at[step], stat_recv.at[step], (grp, level_peer(step)))
    for step in range(1, depth):
        source = lax.rem(level - step + depth, depth)
        arrived(stat_all.at[source], stat_send.at[step], stat_recv.at[step])
    everyone = stat_all[...]
    peak_ref[...] = jnp.max(everyone[:, 1, :share], axis=0)
    spread_ref[...] = jnp.sqrt(jnp.sum(everyone[:, 0, :share], axis=0) / (cells * nodes) + 1e-06)

    write.wait()
    for copy in sent:
        copy.wait_send()


def local(damage, basis_table, train_ids, counts, new_table, new_ids):
    groups, nodes = lax.axis_size("grp"), lax.axis_size("node")
    slots, cells = damage.shape
    rows, terms = new_table.shape
    samples = new_ids.shape[0]
    edge, depth = side_of(groups), nodes // 2
    chunk, block, share = terms // nodes, cells // groups, samples // groups
    stages = min(4, depth)
    lines = depth // stages * chunk
    sizes = (groups, nodes, slots, terms, cells, samples, rows)
    dma = pltpu.SemaphoreType.DMA
    any_space = pl.BlockSpec(memory_space=pl.ANY)
    vmem = pl.BlockSpec(memory_space=pltpu.VMEM)
    return pl.pallas_call(
        functools.partial(kernel, sizes),
        out_shape=(
            jax.ShapeDtypeStruct((share, cells), BF16),
            jax.ShapeDtypeStruct((share,), F32),
            jax.ShapeDtypeStruct((share,), F32),
        ),
        in_specs=[any_space, any_space, vmem, pl.BlockSpec(memory_space=pltpu.SMEM), any_space, vmem],
        out_specs=(any_space, vmem, vmem),
        scratch_shapes=[
            pltpu.VMEM((slots, cells), BF16),
            pltpu.VMEM((slots, terms), BF16),
            pltpu.VMEM((rows, terms), BF16),
            pltpu.VMEM((groups, slots, slots), BF16),
            pltpu.VMEM((groups, chunk, slots), BF16),
            pltpu.VMEM((depth, 2, chunk, slots), BF16),
            pltpu.VMEM((stages, 2, edge, edge, lines, block), BF16),
            pltpu.VMEM((stages, 2, edge - 1, edge, lines, block), BF16),
            pltpu.VMEM((stages, 2, edge, lines, block), BF16),
            pltpu.VMEM((stages, 2, edge - 1, lines, block), BF16),
            pltpu.VMEM((terms, block), BF16),
            pltpu.VMEM((samples // edge, rows), BF16),
            pltpu.VMEM((samples, terms), BF16),
            pltpu.VMEM((edge, edge, share, block), BF16),
            pltpu.VMEM((share, cells), BF16),
            pltpu.VMEM((8, 128), F32),
            pltpu.VMEM((8, 128), F32),
            pltpu.VMEM((depth, 8, 128), F32),
            dma((4,)),
            dma((groups,)), dma((groups,)),
            dma((depth,)), dma((depth,)),
            dma((depth,)), dma((depth,)),
            dma((stages, 2, edge)), dma((stages, 2, edge)),
            dma((stages, 2, edge)), dma((stages, 2, edge)),
            dma((groups,)), dma((groups,)),
            dma((depth,)), dma((depth,)),
        ],
        compiler_params=pltpu.CompilerParams(
            collective_id=0, has_side_effects=True, vmem_limit_bytes=48 * 1024 * 1024
        ),
        name="projection",
    )(damage, basis_table, train_ids.reshape(1, -1), counts, new_table, new_ids.reshape(1, -1))


def solution(mesh):
    placed = (P("grp", "node"), P("grp", None), P("grp"), P(), P(), P())
    return jax.shard_map(
        local,
        mesh=mesh,
        in_specs=placed,
        out_specs=(P("grp", "node"), P("grp"), P("grp")),
        check_vma=False,
    )
```

time: 197 us -> 74.1 us (0.38)
  blocking collectives: 79.6 us -> 0 us
  waiting for transfers between devices: 78.7 us -> 0 us
  Pallas kernels: 0 us -> 65.6 us
  between operations: 14.8 us -> 0.65 us
  other arithmetic: 6.56 us -> 0 us
  starting transfers between devices: 4.46 us -> 0 us
  matrix products: 3.8 us -> 0 us
    pallas_call x0 -> x1, Pallas kernels: none -> 65.6 us  [local(): pl.pallas_call(functools.partial(kernel, sizes), out_shape=(jax.ShapeDtyp...]
    all_to_all x2 -> x0, blocking collectives: 60.5 us -> none  [the longest x1 32.2 us: sent_and_summed(): lax.all_to_all(blocks, axis, split_axis=0, concat_axis=0, tiled=True)]
    all_gather x1 -> x0, waiting for transfers between devices: 52.3 us -> none  [local(): lax.all_gather(basis_table, 'grp', axis=0, tiled=True)]
    all_to_all x1 -> x0, waiting for transfers between devices: 25.8 us -> none  [from_everyone(): lax.all_to_all(jnp.broadcast_to(value[None], (size, *value.shape)), axis,...]
    all_gather x1 -> x0, blocking collectives: 19.1 us -> none  [local(): lax.all_gather(train_ids, 'grp', axis=0, tiled=True)]
    unnamed x6 -> x15, local copies, waits for them, and re-layouts: 0.2 us -> 7.5 us
    gather x2 -> x0, local copies, waits for them, and re-layouts: 4.64 us -> none  [the longest x1 3.94 us: local(): chosen = jnp.take(basis_whole, my_slot_ids, axis=0)]
    all_to_all x1 -> x0, starting transfers between devices: 4.42 us -> none  [from_everyone(): lax.all_to_all(jnp.broadcast_to(value[None], (size, *value.shape)), axis,...]
  transfers between devices with their start and end apart: 2 -> 0, of which waited for: 2 -> 0; matrix products, arithmetic and copies ran while one was open for 2% -> 0% of each run, Pallas kernels for 0% -> 0%
where the time goes in v1:
time: 74.1 us; the launch traced here: 73.8 us
  Pallas kernels  65.6 us (89%)
  local copies, waits for them, and re-layouts  7.5 us (10%)
    pallas_call x1, Pallas kernels, local(): pl.pallas_call(functools.partial(kernel, sizes), out_shape=(jax.ShapeDtyp...  65.6 us
    unnamed x15, local copies, waits for them, and re-layouts  7.5 us

profile of v1, /device:TPU:1, one launch (start us, length us, event | category | flops | bytes accessed | tf_op | source)
XLA Modules:
  0.0 73.8 jit_solution(8389288283351068295)
XLA Ops:
  0.6 0.0 copy-start
  0.6 1.6 %copy-done = bf16[2048,512]{1,0:T(8,128)(2,1)S(1)} copy-done((bf16[2048,512]{1,0:T(8,128)(2,1)S(1)}, bf16[2048,512]{1,0:T(8,128)(2,1)}, u32[]{:S(2)}) %copy-start) | copy-done | bytes 2097176
  2.2 0.0 copy-start.1
  2.2 1.2 %copy-done.1 = bf16[256,2048]{1,0:T(8,128)(2,1)S(1)} copy-done((bf16[256,2048]{1,0:T(8,128)(2,1)S(1)}, bf16[256,2048]{1,0:T(8,128)(2,1)}, u32[]{:S(2)}) %copy-start.1) | copy-done | bytes 1048600
  3.4 0.0 copy-start.2
  3.5 0.9 %copy-done.2 = bf16[256,512]{1,0:T(8,128)(2,1)S(1)} copy-done((bf16[256,512]{1,0:T(8,128)(2,1)S(1)}, bf16[256,512]{1,0:T(8,128)(2,1)}, u32[]{:S(2)}) %copy-start.2) | copy-done | bytes 262168
  4.4 0.0 copy-start.3
  4.4 0.7 copy-done.3
  5.1 0.0 copy-start.4
  5.1 0.7 copy-done.4
  5.8 0.0 copy-start.5
  5.8 0.7 copy-done.5
  6.4 65.6 %projection.1 = (bf16[64,2048]{1,0:T(8,128)(2,1)S(1)}, f32[64]{0:T(128)S(1)}, f32[64]{0:T(128)S(1)}) custom-call(bf16[256,2048]{1,0:T(8,128)(2,1)S(1)} %copy-done.1, bf16[256,512]{1,0:T(8,128)(2,1)S(1)} %copy-done.2, s32[1,256]{1,0:T(1,128)S(1)} %bitcast.3, s32[16]{0:T(128)S(1)} %copy-done.5, bf16[2048,512]{1,0:T(8,128)(2,1)S(1)} %copy-done, ...), custom_call_target="tpu_custom_call" | custom-call | tf_op jit(solution)/shard_map/projection/pallas_call | solution.py:292
  72.1 0.7 copy.12
  72.8 0.5 copy.13
  73.3 0.5 copy.14
Async XLA Ops:
  0.6 1.6 %copy-start = (bf16[2048,512]{1,0:T(8,128)(2,1)S(1)}, bf16[2048,512]{1,0:T(8,128)(2,1)}, u32[]{:S(2)}) copy-start(bf16[2048,512]{1,0:T(8,128)(2,1)} %table_hbm.1) | copy-start | bytes 6291460
  2.2 1.2 %copy-start.1 = (bf16[256,2048]{1,0:T(8,128)(2,1)S(1)}, bf16[256,2048]{1,0:T(8,128)(2,1)}, u32[]{:S(2)}) copy-start(bf16[256,2048]{1,0:T(8,128)(2,1)} %damage_hbm.1) | copy-start | bytes 3145732
  3.4 0.9 %copy-start.2 = (bf16[256,512]{1,0:T(8,128)(2,1)S(1)}, bf16[256,512]{1,0:T(8,128)(2,1)}, u32[]{:S(2)}) copy-start(bf16[256,512]{1,0:T(8,128)(2,1)} %basis_hbm.1) | copy-start | bytes 786436
  4.4 0.7 copy-start.3
  5.1 0.7 copy-start.4
  5.8 0.7 copy-start.5

commit v2 on v1

v2 whole, which is shorter than its diff:
```python
import functools

import jax
import jax.numpy as jnp
from jax import lax
from jax.experimental import pallas as pl
from jax.experimental.pallas import tpu as pltpu
from jax.sharding import PartitionSpec as P

MESH = pl.DeviceIdType.MESH
F32 = jnp.float32
BF16 = jnp.bfloat16


def side_of(count):
    side = 1
    while side * side < count:
        side *= 2
    return side


def near_first(count):
    order = [0]
    for step in range(1, count // 2 + 1):
        order += [step, -step]
    return order[:count]


def stage_plan(window):
    plan, at = [(0, 1)], 1
    while at < window:
        plan.append((at, min(at + 2, window)))
        at += 2
    return plan


def kernel(
    sizes,
    damage_hbm, basis_hbm, ids_hbm, counts_hbm, table_hbm, new_ids_hbm,
    out_ref, stat_ref,
    damage, basis, ids_ref, counts_ref, table, new_ids_ref,
    onehot, parts, weights, partial, first_in, half, second_in,
    coef, pick, chosen, sending, field, stat_out, stat_in, stat_all,
    local_sem, near_sem, far_sem, part_send, part_recv, weight_send, weight_recv,
    first_send, first_recv, second_send, second_recv, field_send, field_recv,
    stat_send, stat_recv, node_send, node_recv,
):
    groups, nodes, slots, terms, cells, samples, rows, window = sizes
    edge = side_of(groups)
    depth = nodes // 2
    chunk = terms // (2 * window)
    block = cells // groups
    share = samples // groups
    plan = stage_plan(window)
    offsets = near_first(window)
    reach = window // 2

    grp = lax.axis_index("grp")
    node = lax.axis_index("node")
    col, row = lax.rem(grp, edge), lax.div(grp, edge)
    level, core = lax.div(node, 2), lax.rem(node, 2)
    twin = level * 2 + (1 - core)

    def place(steps):
        down, along = steps
        return lax.rem(row + down + edge, edge) * edge + lax.rem(col + along + edge, edge)

    def level_peer(step, other=0):
        side = 1 - core if other else core
        return lax.rem(level + step + depth, depth) * 2 + side

    def hops(steps):
        return sum(min(k, edge - k) for k in steps)

    around = sorted(((d, a) for d in range(edge) for a in range(edge) if d or a), key=hops)
    near = sorted({k for k in range(-reach, reach + 1) if k % depth}, key=abs)
    near = [k for i, k in enumerate(near) if k % depth not in [m % depth for m in near[:i]]]
    beside = [k for k in near if abs(k) == 1]

    sent = []

    def send(src, dst, send_sem, recv_sem, to):
        copy = pltpu.make_async_remote_copy(
            src_ref=src, dst_ref=dst, send_sem=send_sem, recv_sem=recv_sem,
            device_id=to, device_id_type=MESH,
        )
        copy.start()
        sent.append(copy)

    def arrived(dst, send_sem, recv_sem):
        pltpu.make_async_remote_copy(
            src_ref=dst, dst_ref=dst, send_sem=send_sem, recv_sem=recv_sem,
            device_id=(grp, twin), device_id_type=MESH,
        ).wait_recv()

    loads = [
        pltpu.make_async_copy(src, dst, local_sem.at[i])
        for i, (src, dst) in enumerate((
            (basis_hbm, basis), (ids_hbm, ids_ref), (counts_hbm, counts_ref), (damage_hbm, damage),
            (table_hbm, table), (new_ids_hbm, new_ids_ref),
        ))
    ]
    loads[0].start()

    barrier = pltpu.get_barrier_semaphore()
    greeted = [(place(steps), node) for steps in reversed(around)]
    greeted += [(grp, level_peer(k)) for k in reversed(near)]
    greeted += [(grp, level_peer(k, 1)) for k in beside] + [(grp, twin)]
    for to in greeted:
        pl.semaphore_signal(barrier, inc=1, device_id=to, device_id_type=MESH)
    for load in loads[1:]:
        load.start()

    index = lax.rem(level, window) * 2 + core
    pick_terms = lax.broadcasted_iota(jnp.int32, (chunk, terms), 1) - index * chunk
    pick_terms = pick_terms == lax.broadcasted_iota(jnp.int32, (chunk, terms), 0)
    pick_terms = jnp.where(pick_terms, 1.0, 0.0).astype(BF16)
    loads[0].wait()
    parts[grp] = lax.dot_general(
        pick_terms, basis[...], (((1,), (1,)), ((), ())), preferred_element_type=F32
    ).astype(BF16)

    pl.semaphore_wait(barrier, len(greeted))

    for steps in reversed(around):
        at = steps[0] * edge + steps[1]
        send(parts.at[grp], parts.at[grp], part_send.at[at], part_recv.at[at], (place(steps), node))
    if depth > window:
        for k in (reach, -reach):
            pl.semaphore_signal(near_sem, inc=1, device_id=(grp, level_peer(k)), device_id_type=MESH)

    loads[1].wait()
    loads[2].wait()
    line = lax.broadcasted_iota(jnp.int32, (slots, slots), 0)
    wanted = jnp.broadcast_to(ids_ref[...], (slots, slots)) - line

    @pl.loop(0, groups)
    def _(g):
        onehot[g] = jnp.where(wanted == g * slots, 1.0, 0.0).astype(BF16)

    counts = counts_ref[...]
    total = jnp.sum(counts, axis=1, keepdims=True).astype(F32)
    which = lax.broadcasted_iota(jnp.int32, counts.shape, 1)
    live = jnp.sum(jnp.where(which == grp, counts, 0), axis=1, keepdims=True)

    mine = jnp.dot(parts[grp], onehot[grp], preferred_element_type=F32)
    for steps in around:
        source = place((-steps[0], -steps[1]))
        at = steps[0] * edge + steps[1]
        arrived(parts.at[source], part_send.at[at], part_recv.at[at])
        mine = mine + jnp.dot(parts[source], onehot[source], preferred_element_type=F32)
    slot = lax.broadcasted_iota(jnp.int32, (chunk, slots), 1)
    weights[0, 0] = jnp.where(slot < live, mine, 0.0).astype(BF16)

    send(weights.at[0, 0], weights.at[0, 1], weight_send.at[0, 1], weight_recv.at[0, 1], (grp, twin))
    for k in range(1, window):
        send(
            weights.at[0, 0], weights.at[k, 0], weight_send.at[k, 0], weight_recv.at[k, 0],
            (grp, level_peer(-offsets[k])),
        )
        if abs(offsets[k]) == 1:
            send(
                weights.at[0, 0], weights.at[k, 1], weight_send.at[k, 1], weight_recv.at[k, 1],
                (grp, level_peer(-offsets[k], 1)),
            )

    def pass_on(stage):
        for k in range(*plan[stage]):
            if k:
                arrived(weights.at[k, 0], weight_send.at[k, 0], weight_recv.at[k, 0])
                if abs(offsets[k]) > 1:
                    send(weights.at[k, 0], weights.at[k, 1], weight_send.at[k, 1], weight_recv.at[k, 1], (grp, twin))

    def lines_of(stage):
        return (plan[stage][1] - plan[stage][0]) * chunk

    def project(stage):
        begin, end = plan[stage]
        lines = lines_of(stage)
        for k in range(begin, end):
            arrived(weights.at[k, 1], weight_send.at[k, 1], weight_recv.at[k, 1])
        left = weights[begin:end].reshape(2 * lines, slots)
        for r in range(edge):
            wide = edge * block
            product = jnp.dot(left, damage[:, r * wide : (r + 1) * wide], preferred_element_type=F32).astype(BF16)
            for c in range(edge):
                piece = product[:, c * block : (c + 1) * block]
                partial[stage, 0, c, r, :lines] = piece[:lines]
                partial[stage, 1, r, c, :lines] = piece[lines:]
        for step in sorted(range(1, edge), key=lambda k: -min(k, edge - k)):
            for side, to in ((0, (0, step)), (1, (step, 0))):
                target = lax.rem((row if side else col) + step, edge)
                send(
                    partial.at[stage, side, target, :, :lines], first_in.at[stage, side, step - 1, :, :lines],
                    first_send.at[stage, side, step], first_recv.at[stage, side, step], (place(to), node),
                )

    def middle(stage):
        lines = lines_of(stage)
        for side, own in ((0, col), (1, row)):
            for step in range(1, edge):
                arrived(
                    first_in.at[stage, side, step - 1, :, :lines],
                    first_send.at[stage, side, step], first_recv.at[stage, side, step],
                )
            for q in range(edge):
                amount = partial[stage, side, own, q, :lines].astype(F32)
                for step in range(1, edge):
                    amount = amount + first_in[stage, side, step - 1, q, :lines].astype(F32)
                half[stage, side, q, :lines] = amount.astype(BF16)
        for step in sorted(range(1, edge), key=lambda k: -min(k, edge - k)):
            for side, to in ((0, (step, 0)), (1, (0, step))):
                target = lax.rem((col if side else row) + step, edge)
                send(
                    half.at[stage, side, target, :lines], second_in.at[stage, side, step - 1, :lines],
                    second_send.at[stage, side, step], second_recv.at[stage, side, step], (place(to), node),
                )

    def finish(stage):
        lines = lines_of(stage)
        begin = plan[stage][0]
        for side, own in ((0, row), (1, col)):
            for step in range(1, edge):
                arrived(
                    second_in.at[stage, side, step - 1, :lines],
                    second_send.at[stage, side, step], second_recv.at[stage, side, step],
                )
            amount = half[stage, side, own, :lines].astype(F32)
            for step in range(1, edge):
                amount = amount + second_in[stage, side, step - 1, :lines].astype(F32)
            amount = (amount / total).astype(BF16)
            for i in range(lines // chunk):
                at = side * (lines // chunk) + i
                k, other = begin + at // 2, at % 2
                owner = lax.rem(level + offsets[k] + depth, window) * 2 + (1 - core if other else core)
                coef[pl.ds(pl.multiple_of(owner * chunk, chunk), chunk), :] = amount[i * chunk : (i + 1) * chunk]

    def choose(part):
        width = samples // edge
        wanted_row = new_ids_ref[:, part * width : (part + 1) * width].astype(F32)
        wanted_row = jnp.broadcast_to(wanted_row, (128, width)).T
        lane = lax.broadcasted_iota(jnp.int32, (width, 128), 1).astype(F32)
        wanted_row = wanted_row - lane
        for q in range(rows // 128):
            pick[:, q * 128 : (q + 1) * 128] = jnp.where(wanted_row == q * 128.0, 1.0, 0.0).astype(BF16)
        chosen[part * width : (part + 1) * width, :] = jnp.dot(
            pick[...], table[...], preferred_element_type=F32
        ).astype(BF16)

    stages = len(plan)
    loads[3].wait()
    project(0)
    pass_on(1)
    loads[4].wait()
    loads[5].wait()
    parts_done = 0
    for stage in range(stages):
        if stage + 1 < stages:
            project(stage + 1)
            if stage + 2 < stages:
                pass_on(stage + 2)
        if parts_done < edge:
            choose(parts_done)
            parts_done += 1
        middle(stage)
        if stage:
            finish(stage - 1)
    while parts_done < edge:
        choose(parts_done)
        parts_done += 1
    if depth > window:
        pl.semaphore_wait(near_sem, 2)
    pl.semaphore_signal(far_sem, inc=1, device_id=(grp, twin), device_id_type=MESH)
    pl.semaphore_wait(far_sem, 1)
    finish(stages - 1)

    def own_stat(values):
        turned = values.T
        return jnp.sum(turned * turned, axis=0, keepdims=True), jnp.max(turned, axis=0, keepdims=True)

    here = pl.ds(pl.multiple_of(grp * block, block), block)
    wide = edge * share
    order = sorted(range(edge), key=lambda k: -min(k, edge - k))
    for r in order:
        to_row = lax.rem(row + r, edge)
        values = jnp.dot(
            chosen[pl.ds(pl.multiple_of(to_row * wide, wide), wide), :], coef[...], preferred_element_type=F32
        )
        square, largest = own_stat(values)
        stat_out[r, 0:1, :] = square
        stat_out[r, 1:2, :] = largest
        sending[r] = values.astype(BF16).reshape(edge, share, block)
        for c in order:
            if r or c:
                at = r * edge + c
                send(stat_out.at[r], stat_in.at[at], stat_send.at[at], stat_recv.at[at], (place((r, c)), node))
    for r in order:
        for c in order:
            to_col = lax.rem(col + c, edge)
            at = r * edge + c
            if at:
                send(sending.at[r, to_col], field.at[:, here], field_send.at[at], field_recv.at[at], (place((r, c)), node))
    field[:, here] = sending[0, col]

    square, largest = stat_out[0, 0:1, :], stat_out[0, 1:2, :]
    for steps in around:
        at = steps[0] * edge + steps[1]
        arrived(stat_in.at[at], stat_send.at[at], stat_recv.at[at])
        square = square + stat_in[at, 0:1, :]
        largest = jnp.maximum(largest, stat_in[at, 1:2, :])
    stat_all[node, 0:1, :] = square
    stat_all[node, 1:2, :] = largest
    for step in sorted(range(depth), key=lambda k: -min(k, depth - k)):
        for other in (0, 1):
            if step or other:
                at = step * 2 + other
                send(
                    stat_all.at[node], stat_all.at[node], node_send.at[at], node_recv.at[at],
                    (grp, level_peer(step, other)),
                )

    for steps in around:
        at = steps[0] * edge + steps[1]
        source = place((-steps[0], -steps[1]))
        there = pl.ds(pl.multiple_of(source * block, block), block)
        arrived(field.at[:, there], field_send.at[at], field_recv.at[at])
    write = pltpu.make_async_copy(field, out_ref, local_sem.at[len(loads)])
    write.start()

    for step in sorted(range(depth), key=lambda k: min(k, depth - k)):
        for other in (0, 1):
            if step or other:
                at = step * 2 + other
                source = level_peer(-step, other)
                arrived(stat_all.at[source], node_send.at[at], node_recv.at[at])
    square, largest = stat_all[0, 0:1, :], stat_all[0, 1:2, :]
    for k in range(1, nodes):
        square = square + stat_all[k, 0:1, :]
        largest = jnp.maximum(largest, stat_all[k, 1:2, :])
    stat_ref[0:1, :] = largest
    stat_ref[1:2, :] = jnp.sqrt(square / (cells * nodes) + 1e-06)

    write.wait()
    for copy in sent:
        copy.wait_send()


def local(damage, basis_table, train_ids, counts, new_table, new_ids):
    groups, nodes = lax.axis_size("grp"), lax.axis_size("node")
    slots, cells = damage.shape
    rows, terms = new_table.shape
    samples = new_ids.shape[0]
    edge, depth = side_of(groups), nodes // 2
    window = min(8, depth)
    chunk, block, share = terms // (2 * window), cells // groups, samples // groups
    stages = len(stage_plan(window))
    lines = 2 * chunk
    sizes = (groups, nodes, slots, terms, cells, samples, rows, window)
    dma = pltpu.SemaphoreType.DMA
    hbm = pl.BlockSpec(memory_space=pl.ANY)
    out, stat = pl.pallas_call(
        functools.partial(kernel, sizes),
        out_shape=(
            jax.ShapeDtypeStruct((share, cells), BF16),
            jax.ShapeDtypeStruct((2, edge * share), F32),
        ),
        in_specs=[hbm] * 6,
        out_specs=(pl.BlockSpec(memory_space=pl.ANY), pl.BlockSpec(memory_space=pltpu.VMEM)),
        scratch_shapes=[
            pltpu.VMEM((slots, cells), BF16),
            pltpu.VMEM((slots, terms), BF16),
            pltpu.VMEM((1, slots), jnp.int32),
            pltpu.VMEM((1, groups), jnp.int32),
            pltpu.VMEM((rows, terms), BF16),
            pltpu.VMEM((1, samples), jnp.int32),
            pltpu.VMEM((groups, slots, slots), BF16),
            pltpu.VMEM((groups, chunk, slots), BF16),
            pltpu.VMEM((window, 2, chunk, slots), BF16),
            pltpu.VMEM((stages, 2, edge, edge, lines, block), BF16),
            pltpu.VMEM((stages, 2, edge - 1, edge, lines, block), BF16),
            pltpu.VMEM((stages, 2, edge, lines, block), BF16),
            pltpu.VMEM((stages, 2, edge - 1, lines, block), BF16),
            pltpu.VMEM((terms, block), BF16),
            pltpu.VMEM((samples // edge, rows), BF16),
            pltpu.VMEM((samples, terms), BF16),
            pltpu.VMEM((edge, edge, share, block), BF16),
            pltpu.VMEM((share, cells), BF16),
            pltpu.VMEM((edge, 2, edge * share), F32),
            pltpu.VMEM((groups, 2, edge * share), F32),
            pltpu.VMEM((nodes, 2, edge * share), F32),
            dma((7,)),
            pltpu.SemaphoreType.REGULAR,
            pltpu.SemaphoreType.REGULAR,
            dma((groups,)), dma((groups,)),
            dma((window, 2)), dma((window, 2)),
            dma((stages, 2, edge)), dma((stages, 2, edge)),
            dma((stages, 2, edge)), dma((stages, 2, edge)),
            dma((groups,)), dma((groups,)),
            dma((groups,)), dma((groups,)),
            dma((nodes,)), dma((nodes,)),
        ],
        compiler_params=pltpu.CompilerParams(
            collective_id=0, has_side_effects=True, vmem_limit_bytes=61950 * 1024
        ),
        name="projection",
    )(damage, basis_table, train_ids.reshape(1, -1), counts.reshape(1, -1), new_table, new_ids.reshape(1, -1))
    at = lax.rem(lax.axis_index("grp"), edge) * share
    stat = lax.dynamic_slice_in_dim(stat, at, share, 1)
    return out, stat[0], stat[1]


def solution(mesh):
    placed = (P("grp", "node"), P("grp", None), P("grp"), P(), P(), P())
    return jax.shard_map(
        local,
        mesh=mesh,
        in_specs=placed,
        out_specs=(P("grp", "node"), P("grp"), P("grp")),
        check_vma=False,
    )
```

time: 74.1 us -> 63.2 us (0.85)
  Pallas kernels: 65.6 us -> 59.4 us
  local copies, waits for them, and re-layouts: 7.5 us -> 2.93 us
    pallas_call x1, Pallas kernels: 65.6 us -> 59.4 us  [local(): pl.pallas_call(functools.partial(kernel, sizes), out_shape=(jax.ShapeDtyp...]
    unnamed x15 -> x1, local copies, waits for them, and re-layouts: 7.5 us -> 1.67 us
    dynamic_slice x0 -> x1, local copies, waits for them, and re-layouts: none -> 0.74 us  [local(): stat = lax.dynamic_slice_in_dim(stat, at, share, 1)]
where the time goes in v2:
time: 63.2 us; the launch traced here: 63 us
  Pallas kernels  59.4 us (94%)
  local copies, waits for them, and re-layouts  2.93 us (5%)
  between operations  0.65 us (1%)
    pallas_call x1, Pallas kernels, local(): pl.pallas_call(functools.partial(kernel, sizes), out_shape=(jax.ShapeDtyp...  59.4 us
    unnamed x1, local copies, waits for them, and re-layouts  1.67 us

profile of v2, /device:TPU:1, one launch (start us, length us, event | category | flops | bytes accessed | tf_op | source)
XLA Modules:
  0.0 63.0 jit_solution(14250089783695189730)
XLA Ops:
  0.6 59.4 %projection.1 = (bf16[64,2048]{1,0:T(8,128)(2,1)}, f32[2,256]{1,0:T(2,128)}) custom-call(bf16[256,2048]{1,0:T(8,128)(2,1)} %damage_hbm.1, bf16[256,512]{1,0:T(8,128)(2,1)} %basis_hbm.1, s32[1,256]{1,0:T(1,128)} %bitcast.8, s32[1,16]{1,0:T(1,128)} %bitcast.9, bf16[2048,512]{1,0:T(8,128)(2,1)} %table_hbm.1, s32[1,1024]{1,0:T(1,128)} %bitcast.7), custom_call_target="tpu_custom_call" | custom-call | tf_op jit(solution)/shard_map/projection/pallas_call | solution.py:361
  60.1 0.7 %constant_dynamic-slice_fusion = f32[2,64]{1,0:T(2,128)S(1)} fusion(f32[2,256]{1,0:T(2,128)} %get-tuple-element.6, s32[]{:T(128)S(6)} %select_n.3), kind=kLoop, calls=%fused_computation.2 | loop fusion | bytes 1028 | tf_op jit(solution)/shard_map/dynamic_slice | solution.py:408
  60.8 0.5 slice_bitcast_fusion
  61.3 1.7 %copy.10 = bf16[64,2048]{1,0:T(8,128)(2,1)} copy(bf16[64,2048]{1,0:T(8,128)(2,1)} %get-tuple-element.12) | data formatting | bytes 524288

commit v3 on v2

--- a/solution.py
+++ b/solution.py
@@ -27,11 +27,8 @@
 
 
 def stage_plan(window):
-    plan, at = [(0, 1)], 1
-    while at < window:
-        plan.append((at, min(at + 2, window)))
-        at += 2
-    return plan
+    cuts = sorted({min(k, window) for k in (0, 1, 3, 7, 11, 15, window)})
+    return list(zip(cuts[:-1], cuts[1:]))
 
 
 def kernel(
@@ -53,7 +50,8 @@
     share = samples // groups
     plan = stage_plan(window)
     offsets = near_first(window)
-    reach = window // 2
+    reach = min(4, depth // 2)
+    relayed = depth > 2 * reach
 
     grp = lax.axis_index("grp")
     node = lax.axis_index("node")
@@ -125,7 +123,7 @@
     for steps in reversed(around):
         at = steps[0] * edge + steps[1]
         send(parts.at[grp], parts.at[grp], part_send.at[at], part_recv.at[at], (place(steps), node))
-    if depth > window:
+    if relayed:
         for k in (reach, -reach):
             pl.semaphore_signal(near_sem, inc=1, device_id=(grp, level_peer(k)), device_id_type=MESH)
 
@@ -137,6 +135,23 @@
     @pl.loop(0, groups)
     def _(g):
         onehot[g] = jnp.where(wanted == g * slots, 1.0, 0.0).astype(BF16)
+
+    def choose(part):
+        width = samples // edge
+        wanted_row = new_ids_ref[:, part * width : (part + 1) * width].astype(F32)
+        wanted_row = jnp.broadcast_to(wanted_row, (128, width)).T
+        lane = lax.broadcasted_iota(jnp.int32, (width, 128), 1).astype(F32)
+        wanted_row = wanted_row - lane
+        for q in range(rows // 128):
+            pick[:, q * 128 : (q + 1) * 128] = jnp.where(wanted_row == q * 128.0, 1.0, 0.0).astype(BF16)
+        chosen[part * width : (part + 1) * width, :] = jnp.dot(
+            pick[...], table[...], preferred_element_type=F32
+        ).astype(BF16)
+
+    loads[4].wait()
+    loads[5].wait()
+    for part in range(edge // 2):
+        choose(part)
 
     counts = counts_ref[...]
     total = jnp.sum(counts, axis=1, keepdims=True).astype(F32)
@@ -154,6 +169,8 @@
 
     send(weights.at[0, 0], weights.at[0, 1], weight_send.at[0, 1], weight_recv.at[0, 1], (grp, twin))
     for k in range(1, window):
+        if relayed and k == 2 * reach:
+            pl.semaphore_wait(near_sem, 2)
         send(
             weights.at[0, 0], weights.at[k, 0], weight_send.at[k, 0], weight_recv.at[k, 0],
             (grp, level_peer(-offsets[k])),
@@ -235,31 +252,17 @@
                 owner = lax.rem(level + offsets[k] + depth, window) * 2 + (1 - core if other else core)
                 coef[pl.ds(pl.multiple_of(owner * chunk, chunk), chunk), :] = amount[i * chunk : (i + 1) * chunk]
 
-    def choose(part):
-        width = samples // edge
-        wanted_row = new_ids_ref[:, part * width : (part + 1) * width].astype(F32)
-        wanted_row = jnp.broadcast_to(wanted_row, (128, width)).T
-        lane = lax.broadcasted_iota(jnp.int32, (width, 128), 1).astype(F32)
-        wanted_row = wanted_row - lane
-        for q in range(rows // 128):
-            pick[:, q * 128 : (q + 1) * 128] = jnp.where(wanted_row == q * 128.0, 1.0, 0.0).astype(BF16)
-        chosen[part * width : (part + 1) * width, :] = jnp.dot(
-            pick[...], table[...], preferred_element_type=F32
-        ).astype(BF16)
-
     stages = len(plan)
     loads[3].wait()
     project(0)
     pass_on(1)
-    loads[4].wait()
-    loads[5].wait()
-    parts_done = 0
+    parts_done = edge // 2
     for stage in range(stages):
         if stage + 1 < stages:
             project(stage + 1)
             if stage + 2 < stages:
                 pass_on(stage + 2)
-        if parts_done < edge:
+        if stage and parts_done < edge:
             choose(parts_done)
             parts_done += 1
         middle(stage)
@@ -268,8 +271,6 @@
     while parts_done < edge:
         choose(parts_done)
         parts_done += 1
-    if depth > window:
-        pl.semaphore_wait(near_sem, 2)
     pl.semaphore_signal(far_sem, inc=1, device_id=(grp, twin), device_id_type=MESH)
     pl.semaphore_wait(far_sem, 1)
     finish(stages - 1)
@@ -337,8 +338,12 @@
     for k in range(1, nodes):
         square = square + stat_all[k, 0:1, :]
         largest = jnp.maximum(largest, stat_all[k, 1:2, :])
-    stat_ref[0:1, :] = largest
-    stat_ref[1:2, :] = jnp.sqrt(square / (cells * nodes) + 1e-06)
+    spread = jnp.sqrt(square / (cells * nodes) + 1e-06)
+    for c in range(edge):
+        @pl.when(col == c)
+        def _(c=c):
+            stat_ref[0:1, :] = largest[:, c * share : (c + 1) * share]
+            stat_ref[1:2, :] = spread[:, c * share : (c + 1) * share]
 
     write.wait()
     for copy in sent:
@@ -351,10 +356,10 @@
     rows, terms = new_table.shape
     samples = new_ids.shape[0]
     edge, depth = side_of(groups), nodes // 2
-    window = min(8, depth)
+    window = depth
     chunk, block, share = terms // (2 * window), cells // groups, samples // groups
     stages = len(stage_plan(window))
-    lines = 2 * chunk
+    lines = max(end - begin for begin, end in stage_plan(window)) * chunk
     sizes = (groups, nodes, slots, terms, cells, samples, rows, window)
     dma = pltpu.SemaphoreType.DMA
     hbm = pl.BlockSpec(memory_space=pl.ANY)
@@ -362,7 +367,7 @@
         functools.partial(kernel, sizes),
         out_shape=(
             jax.ShapeDtypeStruct((share, cells), BF16),
-            jax.ShapeDtypeStruct((2, edge * share), F32),
+            jax.ShapeDtypeStruct((2, share), F32),
         ),
         in_specs=[hbm] * 6,
         out_specs=(pl.BlockSpec(memory_space=pl.ANY), pl.BlockSpec(memory_space=pltpu.VMEM)),
@@ -404,8 +409,6 @@
         ),
         name="projection",
     )(damage, basis_table, train_ids.reshape(1, -1), counts.reshape(1, -1), new_table, new_ids.reshape(1, -1))
-    at = lax.rem(lax.axis_index("grp"), edge) * share
-    stat = lax.dynamic_slice_in_dim(stat, at, share, 1)
     return out, stat[0], stat[1]
 
 

time: 63.2 us -> 64.9 us (1.027)
  Pallas kernels: 59.4 us -> 61.1 us
    pallas_call x1, Pallas kernels: 59.4 us -> 61.1 us  [local(): pl.pallas_call(functools.partial(kernel, sizes), out_shape=(jax.ShapeDtyp...]
    dynamic_slice x1 -> x0, local copies, waits for them, and re-layouts: 0.74 us -> none  [local(): stat = lax.dynamic_slice_in_dim(stat, at, share, 1)]
    squeeze x1, local copies, waits for them, and re-layouts: 0.52 us -> 1.26 us  [local(): return (out, stat[0], stat[1])]
where the time goes in v3:
time: 64.9 us; the launch traced here: 64.7 us
  Pallas kernels  61.1 us (94%)
  local copies, waits for them, and re-layouts  2.93 us (5%)
    pallas_call x1, Pallas kernels, local(): pl.pallas_call(functools.partial(kernel, sizes), out_shape=(jax.ShapeDtyp...  61.1 us
    unnamed x1, local copies, waits for them, and re-layouts  1.67 us

profile of v3, /device:TPU:1, one launch (start us, length us, event | category | flops | bytes accessed | tf_op | source)
XLA Modules:
  0.0 64.7 jit_solution(17133573469923623020)
XLA Ops:
  0.6 61.1 %projection.1 = (bf16[64,2048]{1,0:T(8,128)(2,1)}, f32[2,64]{1,0:T(2,128)}) custom-call(bf16[256,2048]{1,0:T(8,128)(2,1)} %damage_hbm.1, bf16[256,512]{1,0:T(8,128)(2,1)} %basis_hbm.1, s32[1,256]{1,0:T(1,128)} %bitcast.8, s32[1,16]{1,0:T(1,128)} %bitcast.9, bf16[2048,512]{1,0:T(8,128)(2,1)} %table_hbm.1, s32[1,1024]{1,0:T(1,128)} %bitcast.7), custom_call_target="tpu_custom_call" | custom-call | tf_op jit(solution)/shard_map/projection/pallas_call | solution.py:366
  61.8 1.3 %slice_bitcast_fusion = (f32[64]{0:T(128)}, f32[64]{0:T(128)}) fusion(f32[2,64]{1,0:T(2,128)} %get-tuple-element.6), kind=kLoop, calls=%fused_computation | loop fusion | bytes 1024 | tf_op jit(solution)/shard_map/squeeze | solution.py:412
  63.0 1.7 %copy.10 = bf16[64,2048]{1,0:T(8,128)(2,1)} copy(bf16[64,2048]{1,0:T(8,128)(2,1)} %get-tuple-element.12) | data formatting | bytes 524288

commit v4 on v3

--- a/solution.py
+++ b/solution.py
@@ -27,7 +27,7 @@
 
 
 def stage_plan(window):
-    cuts = sorted({min(k, window) for k in (0, 1, 3, 7, 11, 15, window)})
+    cuts = sorted({min(k, 2 * window) for k in (0, 2, 6, 10, 2 * window)})
     return list(zip(cuts[:-1], cuts[1:]))
 
 
@@ -38,7 +38,7 @@
     damage, basis, ids_ref, counts_ref, table, new_ids_ref,
     onehot, parts, weights, partial, first_in, half, second_in,
     coef, pick, chosen, sending, field, stat_out, stat_in, stat_all,
-    local_sem, near_sem, far_sem, part_send, part_recv, weight_send, weight_recv,
+    local_sem, relay_sem, far_sem, part_send, part_recv, weight_send, weight_recv,
     first_send, first_recv, second_send, second_recv, field_send, field_recv,
     stat_send, stat_recv, node_send, node_recv,
 ):
@@ -49,9 +49,12 @@
     block = cells // groups
     share = samples // groups
     plan = stage_plan(window)
+    stages = len(plan)
     offsets = near_first(window)
-    reach = min(4, depth // 2)
-    relayed = depth > 2 * reach
+    reach = min(2, depth // 2)
+    relays = []
+    while (reach << len(relays)) * 2 < depth:
+        relays.append(reach << len(relays))
 
     grp = lax.axis_index("grp")
     node = lax.axis_index("node")
@@ -123,9 +126,17 @@
     for steps in reversed(around):
         at = steps[0] * edge + steps[1]
         send(parts.at[grp], parts.at[grp], part_send.at[at], part_recv.at[at], (place(steps), node))
-    if relayed:
-        for k in (reach, -reach):
-            pl.semaphore_signal(near_sem, inc=1, device_id=(grp, level_peer(k)), device_id_type=MESH)
+    def relay(i):
+        for k in (relays[i], -relays[i]):
+            pl.semaphore_signal(relay_sem.at[i], inc=1, device_id=(grp, level_peer(k)), device_id_type=MESH)
+
+    def hear_relay(i):
+        pl.semaphore_wait(relay_sem.at[i], 2)
+        if i + 1 < len(relays):
+            relay(i + 1)
+
+    if relays:
+        relay(0)
 
     loads[1].wait()
     loads[2].wait()
@@ -150,7 +161,7 @@
 
     loads[4].wait()
     loads[5].wait()
-    for part in range(edge // 2):
+    for part in range(edge):
         choose(part)
 
     counts = counts_ref[...]
@@ -165,37 +176,42 @@
         arrived(parts.at[source], part_send.at[at], part_recv.at[at])
         mine = mine + jnp.dot(parts[source], onehot[source], preferred_element_type=F32)
     slot = lax.broadcasted_iota(jnp.int32, (chunk, slots), 1)
-    weights[0, 0] = jnp.where(slot < live, mine, 0.0).astype(BF16)
-
-    send(weights.at[0, 0], weights.at[0, 1], weight_send.at[0, 1], weight_recv.at[0, 1], (grp, twin))
+    weights[0] = jnp.where(slot < live, mine, 0.0).astype(BF16)
+
+    send(weights.at[0], weights.at[1], weight_send.at[0, 1], weight_recv.at[0, 1], (grp, twin))
     for k in range(1, window):
-        if relayed and k == 2 * reach:
-            pl.semaphore_wait(near_sem, 2)
+        if relays and k == 2 * reach + 1:
+            hear_relay(0)
         send(
-            weights.at[0, 0], weights.at[k, 0], weight_send.at[k, 0], weight_recv.at[k, 0],
+            weights.at[0], weights.at[2 * k], weight_send.at[k, 0], weight_recv.at[k, 0],
             (grp, level_peer(-offsets[k])),
         )
         if abs(offsets[k]) == 1:
             send(
-                weights.at[0, 0], weights.at[k, 1], weight_send.at[k, 1], weight_recv.at[k, 1],
+                weights.at[0], weights.at[2 * k + 1], weight_send.at[k, 1], weight_recv.at[k, 1],
                 (grp, level_peer(-offsets[k], 1)),
             )
 
     def pass_on(stage):
-        for k in range(*plan[stage]):
-            if k:
-                arrived(weights.at[k, 0], weight_send.at[k, 0], weight_recv.at[k, 0])
+        for u in range(*plan[stage]):
+            k = u // 2
+            if u % 2 == 0 and k:
+                arrived(weights.at[2 * k], weight_send.at[k, 0], weight_recv.at[k, 0])
                 if abs(offsets[k]) > 1:
-                    send(weights.at[k, 0], weights.at[k, 1], weight_send.at[k, 1], weight_recv.at[k, 1], (grp, twin))
+                    send(
+                        weights.at[2 * k], weights.at[2 * k + 1], weight_send.at[k, 1], weight_recv.at[k, 1],
+                        (grp, twin),
+                    )
 
     def lines_of(stage):
-        return (plan[stage][1] - plan[stage][0]) * chunk
+        return (plan[stage][1] - plan[stage][0]) * chunk // 2
 
     def project(stage):
         begin, end = plan[stage]
         lines = lines_of(stage)
-        for k in range(begin, end):
-            arrived(weights.at[k, 1], weight_send.at[k, 1], weight_recv.at[k, 1])
+        for u in range(begin, end):
+            if u % 2:
+                arrived(weights.at[u], weight_send.at[u // 2, 1], weight_recv.at[u // 2, 1])
         left = weights[begin:end].reshape(2 * lines, slots)
         for r in range(edge):
             wide = edge * block
@@ -246,31 +262,29 @@
             for step in range(1, edge):
                 amount = amount + second_in[stage, side, step - 1, :lines].astype(F32)
             amount = (amount / total).astype(BF16)
-            for i in range(lines // chunk):
-                at = side * (lines // chunk) + i
-                k, other = begin + at // 2, at % 2
-                owner = lax.rem(level + offsets[k] + depth, window) * 2 + (1 - core if other else core)
-                coef[pl.ds(pl.multiple_of(owner * chunk, chunk), chunk), :] = amount[i * chunk : (i + 1) * chunk]
-
-    stages = len(plan)
+            piece = min(chunk, lines)
+            for i in range(lines // piece):
+                at = side * lines + i * piece
+                u = begin + at // chunk
+                owner = lax.rem(level + offsets[u // 2] + depth, window) * 2 + (1 - core if u % 2 else core)
+                first = owner * chunk + at % chunk
+                coef[pl.ds(pl.multiple_of(first, piece), piece), :] = amount[i * piece : (i + 1) * piece]
+
     loads[3].wait()
-    project(0)
-    pass_on(1)
-    parts_done = edge // 2
+    ahead = min(3, stages)
+    for stage in range(ahead):
+        pass_on(stage)
+        project(stage)
     for stage in range(stages):
-        if stage + 1 < stages:
-            project(stage + 1)
-            if stage + 2 < stages:
-                pass_on(stage + 2)
-        if stage and parts_done < edge:
-            choose(parts_done)
-            parts_done += 1
+        if stage + ahead < stages:
+            pass_on(stage + ahead)
         middle(stage)
+        if stage + ahead < stages:
+            project(stage + ahead)
         if stage:
             finish(stage - 1)
-    while parts_done < edge:
-        choose(parts_done)
-        parts_done += 1
+    for i in range(1 if window > 2 * reach + 1 else 0, len(relays)):
+        hear_relay(i)
     pl.semaphore_signal(far_sem, inc=1, device_id=(grp, twin), device_id_type=MESH)
     pl.semaphore_wait(far_sem, 1)
     finish(stages - 1)
@@ -339,11 +353,11 @@
         square = square + stat_all[k, 0:1, :]
         largest = jnp.maximum(largest, stat_all[k, 1:2, :])
     spread = jnp.sqrt(square / (cells * nodes) + 1e-06)
-    for c in range(edge):
-        @pl.when(col == c)
-        def _(c=c):
-            stat_ref[0:1, :] = largest[:, c * share : (c + 1) * share]
-            stat_ref[1:2, :] = spread[:, c * share : (c + 1) * share]
+    result = (largest[:, :share], spread[:, :share])
+    for c in range(1, edge):
+        mine = slice(c * share, (c + 1) * share)
+        result = (jnp.where(col == c, largest[:, mine], result[0]), jnp.where(col == c, spread[:, mine], result[1]))
+    stat_ref[0:1, :], stat_ref[1:2, :] = result
 
     write.wait()
     for copy in sent:
@@ -356,10 +370,10 @@
     rows, terms = new_table.shape
     samples = new_ids.shape[0]
     edge, depth = side_of(groups), nodes // 2
-    window = depth
+    window = min(8, depth)
     chunk, block, share = terms // (2 * window), cells // groups, samples // groups
     stages = len(stage_plan(window))
-    lines = max(end - begin for begin, end in stage_plan(window)) * chunk
+    lines = max(end - begin for begin, end in stage_plan(window)) * chunk // 2
     sizes = (groups, nodes, slots, terms, cells, samples, rows, window)
     dma = pltpu.SemaphoreType.DMA
     hbm = pl.BlockSpec(memory_space=pl.ANY)
@@ -380,7 +394,7 @@
             pltpu.VMEM((1, samples), jnp.int32),
             pltpu.VMEM((groups, slots, slots), BF16),
             pltpu.VMEM((groups, chunk, slots), BF16),
-            pltpu.VMEM((window, 2, chunk, slots), BF16),
+            pltpu.VMEM((2 * window, chunk, slots), BF16),
             pltpu.VMEM((stages, 2, edge, edge, lines, block), BF16),
             pltpu.VMEM((stages, 2, edge - 1, edge, lines, block), BF16),
             pltpu.VMEM((stages, 2, edge, lines, block), BF16),
@@ -394,7 +408,7 @@
             pltpu.VMEM((groups, 2, edge * share), F32),
             pltpu.VMEM((nodes, 2, edge * share), F32),
             dma((7,)),
-            pltpu.SemaphoreType.REGULAR,
+            pltpu.SemaphoreType.REGULAR((4,)),
             pltpu.SemaphoreType.REGULAR,
             dma((groups,)), dma((groups,)),
             dma((window, 2)), dma((window, 2)),

time: 64.9 us -> 62.4 us (0.961)
  Pallas kernels: 61.1 us -> 58.6 us
    pallas_call x1, Pallas kernels: 61.1 us -> 58.6 us  [local(): pl.pallas_call(functools.partial(kernel, sizes), out_shape=(jax.ShapeDtyp...]
where the time goes in v4:
time: 62.4 us; the launch traced here: 62.2 us
  Pallas kernels  58.6 us (94%)
  local copies, waits for them, and re-layouts  2.93 us (5%)
  between operations  0.64 us (1%)
    pallas_call x1, Pallas kernels, local(): pl.pallas_call(functools.partial(kernel, sizes), out_shape=(jax.ShapeDtyp...  58.6 us
    unnamed x1, local copies, waits for them, and re-layouts  1.67 us
    squeeze x1, local copies, waits for them, and re-layouts, local(): return (out, stat[0], stat[1])  1.26 us

profile of v4, /device:TPU:1, one launch (start us, length us, event | category | flops | bytes accessed | tf_op | source)
XLA Modules:
  0.0 62.2 jit_solution(9250768653426301685)
XLA Ops:
  0.6 58.6 %projection.1 = (bf16[64,2048]{1,0:T(8,128)(2,1)}, f32[2,64]{1,0:T(2,128)}) custom-call(bf16[256,2048]{1,0:T(8,128)(2,1)} %damage_hbm.1, bf16[256,512]{1,0:T(8,128)(2,1)} %basis_hbm.1, s32[1,256]{1,0:T(1,128)} %bitcast.8, s32[1,16]{1,0:T(1,128)} %bitcast.9, bf16[2048,512]{1,0:T(8,128)(2,1)} %table_hbm.1, s32[1,1024]{1,0:T(1,128)} %bitcast.7), custom_call_target="tpu_custom_call" | custom-call | tf_op jit(solution)/shard_map/projection/pallas_call | solution.py:380
  59.3 1.3 %slice_bitcast_fusion = (f32[64]{0:T(128)}, f32[64]{0:T(128)}) fusion(f32[2,64]{1,0:T(2,128)} %get-tuple-element.6), kind=kLoop, calls=%fused_computation | loop fusion | bytes 1024 | tf_op jit(solution)/shard_map/squeeze | solution.py:426
  60.5 1.7 %copy.10 = bf16[64,2048]{1,0:T(8,128)(2,1)} copy(bf16[64,2048]{1,0:T(8,128)(2,1)} %get-tuple-element.12) | data formatting | bytes 524288

commit v5 on v4

--- a/solution.py
+++ b/solution.py
@@ -35,11 +35,11 @@
     sizes,
     damage_hbm, basis_hbm, ids_hbm, counts_hbm, table_hbm, new_ids_hbm,
     out_ref, stat_ref,
-    damage, basis, ids_ref, counts_ref, table, new_ids_ref,
+    damage, far_damage, basis, ids_ref, far_ids, counts_ref, table, new_ids_ref,
     onehot, parts, weights, partial, first_in, half, second_in,
     coef, pick, chosen, sending, field, stat_out, stat_in, stat_all,
     local_sem, relay_sem, far_sem, part_send, part_recv, weight_send, weight_recv,
-    first_send, first_recv, second_send, second_recv, field_send, field_recv,
+    far_send, far_recv, first_send, first_recv, second_send, second_recv, field_send, field_recv,
     stat_send, stat_recv, node_send, node_recv,
 ):
     groups, nodes, slots, terms, cells, samples, rows, window = sizes
@@ -74,6 +74,8 @@
         return sum(min(k, edge - k) for k in steps)
 
     around = sorted(((d, a) for d in range(edge) for a in range(edge) if d or a), key=hops)
+    far = edge // 2
+    first_steps = [k for k in range(1, edge) if k != far]
     near = sorted({k for k in range(-reach, reach + 1) if k % depth}, key=abs)
     near = [k for i, k in enumerate(near) if k % depth not in [m % depth for m in near[:i]]]
     beside = [k for k in near if abs(k) == 1]
@@ -126,6 +128,23 @@
     for steps in reversed(around):
         at = steps[0] * edge + steps[1]
         send(parts.at[grp], parts.at[grp], part_send.at[at], part_recv.at[at], (place(steps), node))
+    def far_copies():
+        copies = []
+        for side, to in ((0, (0, far)), (1, (far, 0))):
+            copies.append((ids_ref, far_ids.at[side], side, place(to)))
+        across = lax.rem(col + far, edge)
+        for q in range(edge):
+            columns = pl.ds(pl.multiple_of((q * edge + across) * block, block), block)
+            copies.append((damage.at[:, columns], far_damage.at[0, :, q * block : (q + 1) * block], 2 + q, place((0, far))))
+        columns = pl.ds(pl.multiple_of(lax.rem(row + far, edge) * edge * block, edge * block), edge * block)
+        copies.append((damage.at[:, columns], far_damage.at[1], 2 + edge, place((far, 0))))
+        return copies
+
+    loads[1].wait()
+    loads[3].wait()
+    for src, dst, at, to in far_copies():
+        send(src, dst, far_send.at[at], far_recv.at[at], (to, node))
+
     def relay(i):
         for k in (relays[i], -relays[i]):
             pl.semaphore_signal(relay_sem.at[i], inc=1, device_id=(grp, level_peer(k)), device_id_type=MESH)
@@ -138,14 +157,17 @@
     if relays:
         relay(0)
 
-    loads[1].wait()
     loads[2].wait()
-    line = lax.broadcasted_iota(jnp.int32, (slots, slots), 0)
-    wanted = jnp.broadcast_to(ids_ref[...], (slots, slots)) - line
-
-    @pl.loop(0, groups)
-    def _(g):
-        onehot[g] = jnp.where(wanted == g * slots, 1.0, 0.0).astype(BF16)
+
+    def build(which, ids):
+        line = lax.broadcasted_iota(jnp.int32, (slots, slots), 0)
+        wanted = jnp.broadcast_to(ids, (slots, slots)) - line
+
+        @pl.loop(0, groups)
+        def _(g):
+            onehot[which, g] = jnp.where(wanted == g * slots, 1.0, 0.0).astype(BF16)
+
+    build(0, ids_ref[...])
 
     def choose(part):
         width = samples // edge
@@ -161,22 +183,36 @@
 
     loads[4].wait()
     loads[5].wait()
-    for part in range(edge):
+    for part in range(edge // 2):
         choose(part)
+    for _, dst, at, _ in far_copies()[:2]:
+        arrived(dst, far_send.at[at], far_recv.at[at])
+        build(1 + at, far_ids[at])
 
     counts = counts_ref[...]
     total = jnp.sum(counts, axis=1, keepdims=True).astype(F32)
     which = lax.broadcasted_iota(jnp.int32, counts.shape, 1)
-    live = jnp.sum(jnp.where(which == grp, counts, 0), axis=1, keepdims=True)
-
-    mine = jnp.dot(parts[grp], onehot[grp], preferred_element_type=F32)
+    owners = (grp, place((0, far)), place((far, 0)))
+    live = [jnp.sum(jnp.where(which == owner, counts, 0), axis=1, keepdims=True) for owner in owners]
+    mid = chunk // 2
+
+    def rows_from(source):
+        return [
+            jnp.dot(parts[source], onehot[0, source], preferred_element_type=F32),
+            jnp.dot(parts[source, :mid], onehot[1, source], preferred_element_type=F32),
+            jnp.dot(parts[source, mid:], onehot[2, source], preferred_element_type=F32),
+        ]
+
+    mine = rows_from(grp)
     for steps in around:
         source = place((-steps[0], -steps[1]))
         at = steps[0] * edge + steps[1]
         arrived(parts.at[source], part_send.at[at], part_recv.at[at])
-        mine = mine + jnp.dot(parts[source], onehot[source], preferred_element_type=F32)
+        mine = [have + more for have, more in zip(mine, rows_from(source))]
     slot = lax.broadcasted_iota(jnp.int32, (chunk, slots), 1)
-    weights[0] = jnp.where(slot < live, mine, 0.0).astype(BF16)
+    weights[0, 0] = jnp.where(slot < live[0], mine[0], 0.0).astype(BF16)
+    weights[0, 1, :mid] = jnp.where(slot[:mid] < live[1], mine[1], 0.0).astype(BF16)
+    weights[0, 1, mid:] = jnp.where(slot[mid:] < live[2], mine[2], 0.0).astype(BF16)
 
     send(weights.at[0], weights.at[1], weight_send.at[0, 1], weight_recv.at[0, 1], (grp, twin))
     for k in range(1, window):
@@ -212,15 +248,17 @@
         for u in range(begin, end):
             if u % 2:
                 arrived(weights.at[u], weight_send.at[u // 2, 1], weight_recv.at[u // 2, 1])
-        left = weights[begin:end].reshape(2 * lines, slots)
+        count = end - begin
+        wide = edge * block
+        left = weights[begin:end, 0].reshape(2 * lines, slots)
         for r in range(edge):
-            wide = edge * block
             product = jnp.dot(left, damage[:, r * wide : (r + 1) * wide], preferred_element_type=F32).astype(BF16)
+            product = product.reshape(count, chunk, wide)
             for c in range(edge):
-                piece = product[:, c * block : (c + 1) * block]
-                partial[stage, 0, c, r, :lines] = piece[:lines]
-                partial[stage, 1, r, c, :lines] = piece[lines:]
-        for step in sorted(range(1, edge), key=lambda k: -min(k, edge - k)):
+                piece = product[:, :, c * block : (c + 1) * block]
+                partial[stage, 0, c, r, :lines] = piece[:, :mid].reshape(lines, block)
+                partial[stage, 1, r, c, :lines] = piece[:, mid:].reshape(lines, block)
+        for step in first_steps:
             for side, to in ((0, (0, step)), (1, (step, 0))):
                 target = lax.rem((row if side else col) + step, edge)
                 send(
@@ -228,17 +266,31 @@
                     first_send.at[stage, side, step], first_recv.at[stage, side, step], (place(to), node),
                 )
 
+    def add_far(stage):
+        begin, end = plan[stage]
+        lines = lines_of(stage)
+        if stage == 0:
+            for _, dst, at, _ in far_copies()[2:]:
+                arrived(dst, far_send.at[at], far_recv.at[at])
+        for side, own, terms_of in ((0, col, slice(0, mid)), (1, row, slice(mid, chunk))):
+            left = weights[begin:end, 1, terms_of].reshape(lines, slots)
+            product = jnp.dot(left, far_damage[side], preferred_element_type=F32)
+            for q in range(edge):
+                amount = partial[stage, side, own, q, :lines].astype(F32) + product[:, q * block : (q + 1) * block]
+                partial[stage, side, own, q, :lines] = amount.astype(BF16)
+
     def middle(stage):
         lines = lines_of(stage)
+        add_far(stage)
         for side, own in ((0, col), (1, row)):
-            for step in range(1, edge):
+            for step in first_steps:
                 arrived(
                     first_in.at[stage, side, step - 1, :, :lines],
                     first_send.at[stage, side, step], first_recv.at[stage, side, step],
                 )
             for q in range(edge):
                 amount = partial[stage, side, own, q, :lines].astype(F32)
-                for step in range(1, edge):
+                for step in first_steps:
                     amount = amount + first_in[stage, side, step - 1, q, :lines].astype(F32)
                 half[stage, side, q, :lines] = amount.astype(BF16)
         for step in sorted(range(1, edge), key=lambda k: -min(k, edge - k)):
@@ -251,7 +303,7 @@
 
     def finish(stage):
         lines = lines_of(stage)
-        begin = plan[stage][0]
+        begin, end = plan[stage]
         for side, own in ((0, row), (1, col)):
             for step in range(1, edge):
                 arrived(
@@ -262,19 +314,18 @@
             for step in range(1, edge):
                 amount = amount + second_in[stage, side, step - 1, :lines].astype(F32)
             amount = (amount / total).astype(BF16)
-            piece = min(chunk, lines)
-            for i in range(lines // piece):
-                at = side * lines + i * piece
-                u = begin + at // chunk
+            for i in range(end - begin):
+                u = begin + i
                 owner = lax.rem(level + offsets[u // 2] + depth, window) * 2 + (1 - core if u % 2 else core)
-                first = owner * chunk + at % chunk
-                coef[pl.ds(pl.multiple_of(first, piece), piece), :] = amount[i * piece : (i + 1) * piece]
-
-    loads[3].wait()
+                first = pl.multiple_of(owner * chunk + side * mid, mid)
+                coef[pl.ds(first, mid), :] = amount[i * mid : (i + 1) * mid]
+
     ahead = min(3, stages)
     for stage in range(ahead):
         pass_on(stage)
         project(stage)
+    for part in range(edge // 2, edge):
+        choose(part)
     for stage in range(stages):
         if stage + ahead < stages:
             pass_on(stage + ahead)
@@ -387,14 +438,16 @@
         out_specs=(pl.BlockSpec(memory_space=pl.ANY), pl.BlockSpec(memory_space=pltpu.VMEM)),
         scratch_shapes=[
             pltpu.VMEM((slots, cells), BF16),
+            pltpu.VMEM((2, slots, edge * block), BF16),
             pltpu.VMEM((slots, terms), BF16),
             pltpu.VMEM((1, slots), jnp.int32),
+            pltpu.VMEM((2, 1, slots), jnp.int32),
             pltpu.VMEM((1, groups), jnp.int32),
             pltpu.VMEM((rows, terms), BF16),
             pltpu.VMEM((1, samples), jnp.int32),
-            pltpu.VMEM((groups, slots, slots), BF16),
+            pltpu.VMEM((3, groups, slots, slots), BF16),
             pltpu.VMEM((groups, chunk, slots), BF16),
-            pltpu.VMEM((2 * window, chunk, slots), BF16),
+            pltpu.VMEM((2 * window, 2, chunk, slots), BF16),
             pltpu.VMEM((stages, 2, edge, edge, lines, block), BF16),
             pltpu.VMEM((stages, 2, edge - 1, edge, lines, block), BF16),
             pltpu.VMEM((stages, 2, edge, lines, block), BF16),
@@ -412,6 +465,7 @@
             pltpu.SemaphoreType.REGULAR,
             dma((groups,)), dma((groups,)),
             dma((window, 2)), dma((window, 2)),
+            dma((edge + 3,)), dma((edge + 3,)),
             dma((stages, 2, edge)), dma((stages, 2, edge)),
             dma((stages, 2, edge)), dma((stages, 2, edge)),
             dma((groups,)), dma((groups,)),

time: 62.4 us -> 64.4 us (1.032)
  Pallas kernels: 58.6 us -> 60.7 us
    pallas_call x1, Pallas kernels: 58.6 us -> 60.7 us  [local(): pl.pallas_call(functools.partial(kernel, sizes), out_shape=(jax.ShapeDtyp...]
where the time goes in v5:
time: 64.4 us; the launch traced here: 64.2 us
  Pallas kernels  60.7 us (94%)
  local copies, waits for them, and re-layouts  2.93 us (5%)
    pallas_call x1, Pallas kernels, local(): pl.pallas_call(functools.partial(kernel, sizes), out_shape=(jax.ShapeDtyp...  60.7 us
    unnamed x1, local copies, waits for them, and re-layouts  1.67 us

profile of v5, /device:TPU:1, one launch (start us, length us, event | category | flops | bytes accessed | tf_op | source)
XLA Modules:
  0.0 64.2 jit_solution(4136211887201901193)
XLA Ops:
  0.6 60.7 %projection.1 = (bf16[64,2048]{1,0:T(8,128)(2,1)}, f32[2,64]{1,0:T(2,128)}) custom-call(bf16[256,2048]{1,0:T(8,128)(2,1)} %damage_hbm.1, bf16[256,512]{1,0:T(8,128)(2,1)} %basis_hbm.1, s32[1,256]{1,0:T(1,128)} %bitcast.8, s32[1,16]{1,0:T(1,128)} %bitcast.9, bf16[2048,512]{1,0:T(8,128)(2,1)} %table_hbm.1, s32[1,1024]{1,0:T(1,128)} %bitcast.7), custom_call_target="tpu_custom_call" | custom-call | tf_op jit(solution)/shard_map/projection/pallas_call | solution.py:431
  61.3 1.3 %slice_bitcast_fusion = (f32[64]{0:T(128)}, f32[64]{0:T(128)}) fusion(f32[2,64]{1,0:T(2,128)} %get-tuple-element.6), kind=kLoop, calls=%fused_computation | loop fusion | bytes 1024 | tf_op jit(solution)/shard_map/squeeze | solution.py:480
  62.6 1.7 %copy.10 = bf16[64,2048]{1,0:T(8,128)(2,1)} copy(bf16[64,2048]{1,0:T(8,128)(2,1)} %get-tuple-element.12) | data formatting | bytes 524288

commit v6 on v4

--- a/solution.py
+++ b/solution.py
@@ -206,6 +206,13 @@
     def lines_of(stage):
         return (plan[stage][1] - plan[stage][0]) * chunk // 2
 
+    def packed(stage, q=None):
+        lines = lines_of(stage)
+        first = edge * plan[stage][0] * chunk // 2
+        if q is None:
+            return slice(first, first + edge * lines)
+        return slice(first + q * lines, first + (q + 1) * lines)
+
     def project(stage):
         begin, end = plan[stage]
         lines = lines_of(stage)
@@ -218,13 +225,13 @@
             product = jnp.dot(left, damage[:, r * wide : (r + 1) * wide], preferred_element_type=F32).astype(BF16)
             for c in range(edge):
                 piece = product[:, c * block : (c + 1) * block]
-                partial[stage, 0, c, r, :lines] = piece[:lines]
-                partial[stage, 1, r, c, :lines] = piece[lines:]
+                partial[0, c, packed(stage, r)] = piece[:lines]
+                partial[1, r, packed(stage, c)] = piece[lines:]
         for step in sorted(range(1, edge), key=lambda k: -min(k, edge - k)):
             for side, to in ((0, (0, step)), (1, (step, 0))):
                 target = lax.rem((row if side else col) + step, edge)
                 send(
-                    partial.at[stage, side, target, :, :lines], first_in.at[stage, side, step - 1, :, :lines],
+                    partial.at[side, target, packed(stage)], first_in.at[side, step - 1, packed(stage)],
                     first_send.at[stage, side, step], first_recv.at[stage, side, step], (place(to), node),
                 )
 
@@ -233,13 +240,13 @@
         for side, own in ((0, col), (1, row)):
             for step in range(1, edge):
                 arrived(
-                    first_in.at[stage, side, step - 1, :, :lines],
+                    first_in.at[side, step - 1, packed(stage)],
                     first_send.at[stage, side, step], first_recv.at[stage, side, step],
                 )
             for q in range(edge):
-                amount = partial[stage, side, own, q, :lines].astype(F32)
+                amount = partial[side, own, packed(stage, q)].astype(F32)
                 for step in range(1, edge):
-                    amount = amount + first_in[stage, side, step - 1, q, :lines].astype(F32)
+                    amount = amount + first_in[side, step - 1, packed(stage, q)].astype(F32)
                 half[stage, side, q, :lines] = amount.astype(BF16)
         for step in sorted(range(1, edge), key=lambda k: -min(k, edge - k)):
             for side, to in ((0, (step, 0)), (1, (0, step))):
@@ -395,8 +402,8 @@
             pltpu.VMEM((groups, slots, slots), BF16),
             pltpu.VMEM((groups, chunk, slots), BF16),
             pltpu.VMEM((2 * window, chunk, slots), BF16),
-            pltpu.VMEM((stages, 2, edge, edge, lines, block), BF16),
-            pltpu.VMEM((stages, 2, edge - 1, edge, lines, block), BF16),
+            pltpu.VMEM((2, edge, edge * terms // 2, block), BF16),
+            pltpu.VMEM((2, edge - 1, edge * terms // 2, block), BF16),
             pltpu.VMEM((stages, 2, edge, lines, block), BF16),
             pltpu.VMEM((stages, 2, edge - 1, lines, block), BF16),
             pltpu.VMEM((terms, block), BF16),

time: 62.4 us -> 62.4 us (level)
  no operation moved by 1% of the time
where the time goes in v6:
time: 62.4 us; the launch traced here: 62.2 us
  Pallas kernels  58.6 us (94%)
  local copies, waits for them, and re-layouts  2.93 us (5%)
  between operations  0.64 us (1%)
    pallas_call x1, Pallas kernels, local(): pl.pallas_call(functools.partial(kernel, sizes), out_shape=(jax.ShapeDtyp...  58.6 us
    unnamed x1, local copies, waits for them, and re-layouts  1.67 us
    squeeze x1, local copies, waits for them, and re-layouts, local(): return (out, stat[0], stat[1])  1.26 us

profile of v6, /device:TPU:1, one launch (start us, length us, event | category | flops | bytes accessed | tf_op | source)
XLA Modules:
  0.0 62.2 jit_solution(17148074676977428287)
XLA Ops:
  0.6 58.6 %projection.1 = (bf16[64,2048]{1,0:T(8,128)(2,1)}, f32[2,64]{1,0:T(2,128)}) custom-call(bf16[256,2048]{1,0:T(8,128)(2,1)} %damage_hbm.1, bf16[256,512]{1,0:T(8,128)(2,1)} %basis_hbm.1, s32[1,256]{1,0:T(1,128)} %bitcast.8, s32[1,16]{1,0:T(1,128)} %bitcast.9, bf16[2048,512]{1,0:T(8,128)(2,1)} %table_hbm.1, s32[1,1024]{1,0:T(1,128)} %bitcast.7), custom_call_target="tpu_custom_call" | custom-call | tf_op jit(solution)/shard_map/projection/pallas_call | solution.py:387
  59.3 1.3 %slice_bitcast_fusion = (f32[64]{0:T(128)}, f32[64]{0:T(128)}) fusion(f32[2,64]{1,0:T(2,128)} %get-tuple-element.6), kind=kLoop, calls=%fused_computation | loop fusion | bytes 1024 | tf_op jit(solution)/shard_map/squeeze | solution.py:433
  60.5 1.7 %copy.10 = bf16[64,2048]{1,0:T(8,128)(2,1)} copy(bf16[64,2048]{1,0:T(8,128)(2,1)} %get-tuple-element.12) | data formatting | bytes 524288
